TPU v7x, 512 devices: a whole 4x8x8 slice. The times are simulated.
512 devices in a mesh: space: 16 (over y, x_lo), mode: 32 (over x_hi, z, core).
Axes of the slice: x: 4 (x_hi: 2, x_lo: 2; x = x_hi * 2 + x_lo), y: 8, z: 8, core: 2. Of those that a mesh axis runs over, the one named last changes fastest.
Arguments:
- members: bfloat16 [80, 524288], P(None, ('space', 'mode')), may hold values from -6 to 6
- modes: bfloat16 [128, 524288], P('mode', 'space'), may hold values from -6 to 6
- obs_weights: bfloat16 [2048, 128, 128], P('space'), may hold values from -0.5 to 0.5
- innovations: float32 [2048, 128], P('space'), may hold values from -6 to 6
- tile_start: int32 [2048], P('space'), may hold values from 0 to 32896, as said below
Outputs:
- increment: float32 [524288], P(('space', 'mode'))
- coefficients: float32 [80, 128], P(None, 'mode')
Inputs may be any that keep to these rules, and one draw needn't show every extreme that they name: In every horizontal tile the first block's tile_start lies in 0 .. 64 and the last block's in 32832 .. 32896; the first block of the slab starts at 0 and the last at 32896.
All inputs are finite; a program needn't handle non-finite values.
Results may differ from a plain program's by a relative error of at most 0.0003.
Values may be sent and summed in bfloat16 or wider, within the bound.
No kernel may reach another device: no remote copies, remote signals or barrier semaphores. Data moves between devices by JAX's collectives and lax.ppermute only.
A program may use at most 64 MiB of HBM per device.

v0:
```python
import functools

import jax
import jax.numpy as jnp
import numpy as np
from jax import lax
from jax.experimental import pallas as pl
from jax.experimental.pallas import tpu as pltpu
from jax.sharding import Mesh
from jax.sharding import PartitionSpec as P

MEMBERS = 80
MODE_DEV = 4
MODES = 128
CELLS_DEV = 32768
TILE = 128
BLK_DEV = 128
OWN = 1024
OWN_TILES = OWN // TILE
LANES = 128
SUBLANES = 8
GROUP = 4
PIECE = 16
VMEM = pl.BlockSpec(memory_space=pltpu.VMEM)
SMALL = pltpu.CompilerParams(vmem_limit_bytes=12 * 2**20)
MODE = ("xhi", "zhi", "zlo", "core")
SPACE = ("y", "xlo")
NEAR = ("xlo", "xhi", "zlo", "core")
FAR = ("y", "zhi")
FIRST = {NEAR: {"xhi": 1, "zlo": 1}, FAR: {"y": 4, "zhi": 2}, MODE: {"xhi": 1, "zhi": 2}}


def mode_index():
    at = lax.axis_index(MODE[0])
    for axis in MODE[1:]:
        at = at * lax.axis_size(axis) + lax.axis_index(axis)
    return at


def split2(x):
    high = x.astype(jnp.bfloat16)
    return high, (x - high.astype(jnp.float32)).astype(jnp.bfloat16)


def field_kernel(last, begin_ref, innov_ref, obs_ref, own_ref, halo_ref, start_ref, ids, rows, held, acc, halo, begin_sem, row_sem, sems):
    m = mode_index()
    begin = pltpu.make_async_copy(begin_ref, start_ref, begin_sem)
    begin.start()
    pieces = [
        pltpu.make_async_copy(obs_ref.at[pl.ds(i * PIECE, PIECE)], held.at[pl.ds(i * PIECE, PIECE)], sems.at[i])
        for i in range(BLK_DEV // PIECE)
    ]
    pieces.append(pltpu.make_async_copy(innov_ref, rows, row_sem))
    for piece in pieces:
        piece.start()
    base = m * OWN
    first = jnp.where(m == 0, CELLS_DEV + TILE, 0)
    edge = (m == 0) | (m == last)
    acc[...] = jnp.zeros_like(acc)
    halo[...] = jnp.zeros_like(halo)
    begin.wait()

    def scan(b, count):
        start = start_ref[b]
        place = start - base
        far = start - first
        ids[count] = b
        hit = ((place > 0) & (place < OWN + TILE)) | (edge & (far > -TILE) & (far < TILE))
        return count + jnp.where(hit, 1, 0)

    count = lax.fori_loop(0, BLK_DEV, scan, jnp.int32(0), unroll=16)
    lane = lax.broadcasted_iota(jnp.int32, (1, LANES), 1)
    for piece in pieces:
        piece.wait()

    def add(g, carry):
        found = []
        for u in range(GROUP):
            i = g * GROUP + u
            valid = i < count
            b = jnp.where(valid, ids[i], 0)
            start = start_ref[b]
            row = rows[pl.ds(b, 1), :]
            high = row.astype(jnp.bfloat16).astype(jnp.float32)
            mid = (row - high).astype(jnp.bfloat16).astype(jnp.float32)
            low = row - high - mid
            parts = jnp.concatenate([high, mid, low, jnp.zeros((SUBLANES - 3, LANES), jnp.float32)], axis=0)
            adj = jnp.dot(parts.astype(jnp.bfloat16), held[b], preferred_element_type=jnp.float32)
            adj = adj + pltpu.roll(adj, SUBLANES - 1, 0) + pltpu.roll(adj, SUBLANES - 2, 0)
            off = lax.bitwise_and(start, TILE - 1)
            rolled = pltpu.roll(adj, off, 1)[0:1, :]
            front = jnp.where(lane >= off, rolled, 0.0)
            back = jnp.where(lane < off, rolled, 0.0)
            found.append((valid, start - base, start - first, front, back))
        for valid, place, far, front, back in found:

            @pl.when(valid & (place > 0) & (place < OWN + TILE))
            def _():
                seg = lax.shift_right_logical(place, 7)
                acc[pl.ds(seg, 1), :] += front
                acc[pl.ds(seg + 1, 1), :] += back

            @pl.when(valid & edge & (far > -TILE) & (far < TILE))
            def _():
                halo[...] += jnp.where(far >= 0, front, back)

        return carry

    lax.fori_loop(0, lax.shift_right_logical(count + GROUP - 1, 2), add, 0)
    own_ref[...] = acc[1 : 1 + OWN_TILES, :]
    halo_ref[...] = halo[...]


def field(tile_start, innovations, obs_weights, last):
    kept = [pltpu.with_memory_space_constraint(x, pltpu.HBM) for x in (tile_start, innovations, obs_weights)]
    return pl.pallas_call(
        functools.partial(field_kernel, last),
        out_shape=(
            jax.ShapeDtypeStruct((OWN_TILES, LANES), jnp.float32),
            jax.ShapeDtypeStruct((1, LANES), jnp.float32),
        ),
        in_specs=[pl.BlockSpec(memory_space=pltpu.HBM)] * 3,
        out_specs=(VMEM, VMEM),
        scratch_shapes=[
            pltpu.SMEM((BLK_DEV,), jnp.int32),
            pltpu.SMEM((BLK_DEV + GROUP,), jnp.int32),
            pltpu.VMEM((BLK_DEV, LANES), jnp.float32),
            pltpu.VMEM((BLK_DEV, TILE, TILE), jnp.bfloat16),
            pltpu.VMEM((2 * SUBLANES, LANES), jnp.float32),
            pltpu.VMEM((1, LANES), jnp.float32),
            pltpu.SemaphoreType.DMA,
            pltpu.SemaphoreType.DMA,
            pltpu.SemaphoreType.DMA((BLK_DEV // PIECE,)),
        ],
        compiler_params=SMALL,
        cost_estimate=pl.CostEstimate(flops=2**22, bytes_accessed=2**22, transcendentals=0),
        name="field",
    )(*kept)


def lay_kernel(modes_ref, out_ref, sems):
    part = modes_ref.shape[1] // 4
    copies = [
        pltpu.make_async_copy(
            modes_ref.at[:, pl.ds(q * part, part)], out_ref.at[:, pl.ds((3 - q) * part, part)], sems.at[q]
        )
        for q in range(4)
    ]
    for copy in copies:
        copy.start()
    for copy in copies:
        copy.wait()


def lay(modes):
    return pl.pallas_call(
        lay_kernel,
        out_shape=jax.ShapeDtypeStruct(modes.shape, modes.dtype),
        in_specs=[pl.BlockSpec(memory_space=pltpu.HBM)],
        out_specs=VMEM,
        scratch_shapes=[pltpu.SemaphoreType.DMA((4,))],
        compiler_params=SMALL,
        name="lay",
    )(pltpu.with_memory_space_constraint(modes, pltpu.HBM))


def project_kernel(last, own_ref, halo_ref, members_ref, modes_ref, out_ref):
    m = mode_index()
    halo = halo_ref[...]
    row = lax.broadcasted_iota(jnp.int32, (OWN_TILES, LANES), 0)
    takes = ((row == 0) & (m == 0)) | ((row == OWN_TILES - 1) & (m == last))
    weights = own_ref[...] + jnp.where(takes, halo, 0.0)
    contract = (((1,), (1,)), ((), ()))
    highs, lows = [], []
    for j in range(OWN_TILES):
        cells = slice(j * TILE, (j + 1) * TILE)
        high, low = split2(members_ref[:, cells].astype(jnp.float32) * weights[j : j + 1, :])
        highs.append(high)
        lows.append(low)
    modes = modes_ref[...]
    total = lax.dot_general(jnp.concatenate(highs, 1), modes, contract, preferred_element_type=jnp.float32)
    total += lax.dot_general(jnp.concatenate(lows, 1), modes, contract, preferred_element_type=jnp.float32)
    out_ref[...] = total


def project(own, halo, members, modes, last):
    return pl.pallas_call(
        functools.partial(project_kernel, last),
        out_shape=jax.ShapeDtypeStruct((MEMBERS, MODES), jnp.float32),
        in_specs=[VMEM] * 4,
        out_specs=VMEM,
        compiler_params=SMALL,
        name="project",
    )(own, halo, members, modes)


def finish_kernel(total_count, coeff_ref, members_ref, modes_ref, inc_ref, own_ref, turned):
    m = mode_place()
    coeff = coeff_ref[...]
    high, low = split2(coeff)
    modes = modes_ref[...]
    mixed = jnp.dot(high, modes, preferred_element_type=jnp.float32)
    mixed += jnp.dot(low, modes, preferred_element_type=jnp.float32)
    spread = jnp.sum(jnp.sum(coeff * coeff, axis=0, keepdims=True), axis=1, keepdims=True)
    factor = lax.rsqrt(1.0 + spread / total_count)
    turned[...] = coeff.T
    own_ref[...] = turned[pl.ds(m * MODE_DEV, MODE_DEV), :]
    mixed = mixed * members_ref[...].astype(jnp.float32)
    summed = jnp.sum(mixed, axis=0, keepdims=True) * (factor / (MEMBERS - 1))
    for j in range(OWN_TILES):
        inc_ref[j : j + 1, :] = summed[:, j * TILE : (j + 1) * TILE]


def finish(coeff, members, modes):
    return pl.pallas_call(
        functools.partial(finish_kernel, MEMBERS * MODES),
        out_shape=(
            jax.ShapeDtypeStruct((OWN_TILES, LANES), jnp.float32),
            jax.ShapeDtypeStruct((MODE_DEV, MEMBERS), jnp.float32),
        ),
        in_specs=[VMEM] * 3,
        out_specs=(VMEM, VMEM),
        scratch_shapes=[pltpu.VMEM((MODES, MEMBERS), jnp.float32)],
        compiler_params=SMALL,
        name="finish",
    )(coeff, members, modes)


def places(axis):
    sizes = [lax.axis_size(a) for a in axis]
    order = np.arange(np.prod(sizes)).reshape(sizes)
    for d, a in enumerate(axis):
        order = np.roll(order, -FIRST[axis].get(a, 0), axis=d)
    return [[int(place) for place in order.reshape(-1)]]


def mode_place():
    at = 0
    for axis in MODE:
        size = lax.axis_size(axis)
        at = at * size + lax.rem(lax.axis_index(axis) + (size - FIRST[MODE].get(axis, 0)), size)
    return at


def exchange(x, axis):
    return lax.all_to_all(x, axis, split_axis=0, concat_axis=0, axis_index_groups=places(axis), tiled=True)


def everywhere(x, axis):
    return exchange(jnp.broadcast_to(x[None], (lax.axis_size(axis),) + x.shape), axis)


def on_device(members, modes, obs_weights, innovations, tile_start):
    mode_count = lax.axis_size(MODE)
    space_count = lax.axis_size(SPACE)
    last = mode_count - 1
    laid = lay(modes)
    all_modes = lax.all_to_all(
        laid, MODE, split_axis=1, concat_axis=0, axis_index_groups=places(MODE), tiled=True
    )
    own, halo = field(tile_start, innovations, obs_weights, last)
    route = []
    for s in range(space_count):
        behind, ahead = (s - 1) % space_count, (s + 1) % space_count
        route.append((s * mode_count, ahead * mode_count))
        route.append((s * mode_count + last, behind * mode_count + last))
    halo = lax.ppermute(halo, SPACE + MODE, route)
    terms = project(own, halo, members, all_modes, last)
    part = jnp.sum(exchange(terms.reshape(lax.axis_size(NEAR), 1, -1), NEAR), axis=0)
    part = jnp.sum(everywhere(part, FAR), axis=0)
    coeff = everywhere(part, NEAR)
    increment, own_coeff = finish(coeff.reshape(MEMBERS, MODES), members, all_modes)
    return increment.reshape(OWN), own_coeff.T


def solution(mesh):
    finer = Mesh(mesh.devices.reshape(8, 2, 2, 4, 2, 2), SPACE + MODE)
    in_specs = (P(None, SPACE + MODE), P(MODE, SPACE), P(SPACE, None, None), P(SPACE, None), P(SPACE))
    out_specs = (P(SPACE + MODE), P(None, MODE))
    return jax.shard_map(
        on_device, mesh=finer, in_specs=in_specs, out_specs=out_specs, check_vma=False
    )
```

profile of v0, /device:TPU:1, one launch (start us, length us, event | category | flops | bytes accessed | tf_op | source)
XLA Modules:
  0.0 63.4 jit_solution(2012354283345939599)
XLA Ops:
  0.6 0.0 copy-start
  0.6 1.7 %lay.1 = bf16[4,32768]{1,0:T(4,128)(2,1)} custom-call(bf16[4,32768]{1,0:T(4,128)(2,1)} %modes_ref.1), custom_call_target="tpu_custom_call" | custom-call | tf_op jit(solution)/shard_map/lay/pallas_call | solution.py:156
  2.3 17.4 %all-to-all-start = ((bf16[4,32,1024]{2,0,1:T(4,128)(2,1)}), bf16[4,32,1024]{2,0,1:T(4,128)(2,1)S(1)}, u32[]{:S(2)}, u32[]{:S(2)}) async-start(bf16[4,32,1024]{2,0,1:T(4,128)(2,1)} %bitcast), calls=%async_computation | async-start | bytes 524288 | tf_op jit(solution)/shard_map/all_to_all | solution.py:258
  19.7 2.5 %field.1 = (f32[8,128]{1,0:T(8,128)S(1)}, f32[1,128]{1,0:T(1,128)S(1)}) custom-call(s32[128]{0:T(128)} %begin_ref.1, f32[128,128]{1,0:T(8,128)} %innov_ref.1, bf16[128,128,128]{2,1,0:T(8,128)(2,1)} %obs_ref.1), custom_call_target="tpu_custom_call" | custom-call | flops 4194304 | bytes 4194304 | tf_op jit(solution)/shard_map/field/pallas_call | solution.py:116
  22.2 0.7 %collective-permute-start = (f32[1,128]{1,0:T(1,128)S(1)}, f32[1,128]{1,0:T(1,128)S(1)}, u32[]{:S(2)}, u32[]{:S(2)}) collective-permute-start(f32[1,128]{1,0:T(1,128)S(1)} %get-tuple-element.7), channel_id=1, source_target_pairs={{0,32},{31,511},{32,64},{63,31},{64,96},{95,63},{96,128},{127,95},... | collective-permute-start | bytes 1544 | tf_op jit(solution)/shard_map/ppermute | solution.py:267
  22.9 3.9 %all-to-all-done = bf16[4,32,1024]{2,0,1:T(4,128)(2,1)S(1)} async-done(((bf16[4,32,1024]{2,0,1:T(4,128)(2,1)}), bf16[4,32,1024]{2,0,1:T(4,128)(2,1)S(1)}, u32[]{:S(2)}, u32[]{:S(2)}) %all-to-all-start) | async-done | bytes 262176 | tf_op jit(solution)/shard_map/all_to_all | solution.py:258
  26.8 0.1 all_to_all.26.modes_ref
  26.8 0.0 collective-permute-done.halo_ref
  26.9 0.0 copy-done
  26.9 0.3 project.1
  27.2 11.0 %all_to_all.34 = f32[16,1,640]{2,1,0:T(1,128)S(1)} all-to-all(f32[16,1,640]{2,1,0:T(1,128)S(1)} %bitcast.7), channel_id=1, replica_groups={{18,19,16,17,2,3,0,1,50,51,48,49,34,35,32,33},{22,23,20,21,6,7,4,5,54,5..., dimensions={0} | all-to-all | bytes 81920 | tf_op jit(solution)/shard_map/all_to_all | solution.py:246
  38.3 14.4 %all_to_all.35 = f32[32,1,640]{2,1,0:T(1,128)S(1)} all-to-all(f32[32,1,640]{2,1,0:T(1,128)S(1)} %broadcast_in_dim.4), channel_id=1, replica_groups={{264,268,256,260,328,332,320,324,392,396,384,388,456,460,448,452,8,12,0..., dimensions={0} | all-to-all | bytes 163840 | tf_op jit(solution)/shard_map/all_to_all | solution.py:246
  52.6 0.1 reduce_sum.19
  52.7 9.8 %all_to_all.36 = f32[16,1,640]{2,1,0:T(1,128)S(1)} all-to-all(f32[16,1,640]{2,1,0:T(1,128)S(1)} %broadcast_in_dim.5), channel_id=1, replica_groups={{18,19,16,17,2,3,0,1,50,51,48,49,34,35,32,33},{22,23,20,21,6,7,4,5,54,5..., dimensions={0} | all-to-all | bytes 81920 | tf_op jit(solution)/shard_map/all_to_all | solution.py:246
  62.5 0.8 %finish.1 = (f32[8,128]{1,0:T(8,128)}, f32[4,80]{1,0:T(4,128)}) custom-call(f32[80,128]{1,0:T(8,128)S(1)} %bitcast.6, bf16[80,1024]{1,0:T(8,128)(2,1)S(1)} %copy-done, bf16[128,1024]{1,0:T(8,128)(2,1)S(1)} %all_to_all.26.modes_ref), custom_call_target="tpu_custom_call" | custom-call | tf_op jit(solution)/shard_map/finish/pallas_call | solution.py:215
  (3 shorter events, 0.1 us)
Async XLA Ops:
  0.6 26.2 %copy-start = (bf16[80,1024]{1,0:T(8,128)(2,1)S(1)}, bf16[80,1024]{1,0:T(8,128)(2,1)}, u32[]{:S(2)}) copy-start(bf16[80,1024]{1,0:T(8,128)(2,1)} %members_ref.3) | copy-start | bytes 491524
  2.3 24.4 %all-to-all-start = ((bf16[4,32,1024]{2,0,1:T(4,128)(2,1)}), bf16[4,32,1024]{2,0,1:T(4,128)(2,1)S(1)}, u32[]{:S(2)}, u32[]{:S(2)}) async-start(bf16[4,32,1024]{2,0,1:T(4,128)(2,1)} %bitcast), calls=%async_computation | async-start | bytes 524288 | tf_op jit(solution)/shard_map/all_to_all | solution.py:258
  22.2 4.6 %collective-permute-start = (f32[1,128]{1,0:T(1,128)S(1)}, f32[1,128]{1,0:T(1,128)S(1)}, u32[]{:S(2)}, u32[]{:S(2)}) collective-permute-start(f32[1,128]{1,0:T(1,128)S(1)} %get-tuple-element.7), channel_id=1, source_target_pairs={{0,32},{31,511},{32,64},{63,31},{64,96},{95,63},{96,128},{127,95},... | collective-permute-start | bytes 1544 | tf_op jit(solution)/shard_map/ppermute | solution.py:267
where the time goes:
time: 63.7 us; the launch traced here: 63.4 us
  blocking collectives  35.2 us (55%)
  starting transfers between devices  18.1 us (28%)
  Pallas kernels  5.32 us (8%)
  waiting for transfers between devices  3.88 us (6%)
  between operations  0.71 us (1%)
    all_to_all x3, blocking collectives, exchange(): lax.all_to_all(x, axis, split_axis=0, concat_axis=0, axis_index_groups=pl...  35.2 us
    all_to_all x1, starting transfers between devices, on_device(): lax.all_to_all(laid, MODE, split_axis=1, concat_axis=0, axis_index_groups...  17.4 us
    all_to_all x1, waiting for transfers between devices, on_device(): lax.all_to_all(laid, MODE, split_axis=1, concat_axis=0, axis_index_groups...  3.87 us
    pallas_call x1, Pallas kernels, field(): pl.pallas_call(functools.partial(field_kernel, last), out_shape=(jax.Shap...  2.48 us
    pallas_call x1, Pallas kernels, lay(): pl.pallas_call(lay_kernel, out_shape=jax.ShapeDtypeStruct(modes.shape, mo...  1.7 us
  transfers between devices with their start and end apart: 2, of which 1 were waited for; matrix products, arithmetic and copies ran while one was open for 0% of the time, Pallas kernels for 4%

commit v1 on v0

--- a/solution.py
+++ b/solution.py
@@ -42,7 +42,7 @@
     return high, (x - high.astype(jnp.float32)).astype(jnp.bfloat16)
 
 
-def field_kernel(last, begin_ref, innov_ref, obs_ref, own_ref, halo_ref, start_ref, ids, rows, held, acc, halo, begin_sem, row_sem, sems):
+def find_field(last, begin_ref, innov_ref, obs_ref, own_ref, halo_ref, start_ref, ids, rows, held, acc, halo, begin_sem, row_sem, sems):
     m = mode_index()
     begin = pltpu.make_async_copy(begin_ref, start_ref, begin_sem)
     begin.start()
@@ -111,57 +111,85 @@
     halo_ref[...] = halo[...]
 
 
-def field(tile_start, innovations, obs_weights, last):
-    kept = [pltpu.with_memory_space_constraint(x, pltpu.HBM) for x in (tile_start, innovations, obs_weights)]
-    return pl.pallas_call(
-        functools.partial(field_kernel, last),
-        out_shape=(
-            jax.ShapeDtypeStruct((OWN_TILES, LANES), jnp.float32),
-            jax.ShapeDtypeStruct((1, LANES), jnp.float32),
-        ),
-        in_specs=[pl.BlockSpec(memory_space=pltpu.HBM)] * 3,
-        out_specs=(VMEM, VMEM),
-        scratch_shapes=[
-            pltpu.SMEM((BLK_DEV,), jnp.int32),
-            pltpu.SMEM((BLK_DEV + GROUP,), jnp.int32),
-            pltpu.VMEM((BLK_DEV, LANES), jnp.float32),
-            pltpu.VMEM((BLK_DEV, TILE, TILE), jnp.bfloat16),
-            pltpu.VMEM((2 * SUBLANES, LANES), jnp.float32),
-            pltpu.VMEM((1, LANES), jnp.float32),
-            pltpu.SemaphoreType.DMA,
-            pltpu.SemaphoreType.DMA,
-            pltpu.SemaphoreType.DMA((BLK_DEV // PIECE,)),
-        ],
-        compiler_params=SMALL,
-        cost_estimate=pl.CostEstimate(flops=2**22, bytes_accessed=2**22, transcendentals=0),
-        name="field",
-    )(*kept)
-
-
-def lay_kernel(modes_ref, out_ref, sems):
+def waits_long():
+    return lax.axis_index("zhi") < lax.axis_size("zhi") // 2
+
+
+def early_kernel(last, modes_ref, begin_ref, innov_ref, obs_ref, laid_ref, own_ref, halo_ref, lay_sems, *scratch):
     part = modes_ref.shape[1] // 4
     copies = [
         pltpu.make_async_copy(
-            modes_ref.at[:, pl.ds(q * part, part)], out_ref.at[:, pl.ds((3 - q) * part, part)], sems.at[q]
+            modes_ref.at[:, pl.ds(q * part, part)], laid_ref.at[:, pl.ds((3 - q) * part, part)], lay_sems.at[q]
         )
         for q in range(4)
     ]
     for copy in copies:
         copy.start()
+
+    @pl.when(waits_long())
+    def _():
+        find_field(last, begin_ref, innov_ref, obs_ref, own_ref, halo_ref, *scratch)
+
     for copy in copies:
         copy.wait()
 
 
-def lay(modes):
+def late_kernel(last, begin_ref, innov_ref, obs_ref, early_own_ref, early_halo_ref, own_ref, halo_ref, *scratch):
+    @pl.when(waits_long())
+    def _():
+        own_ref[...] = early_own_ref[...]
+        halo_ref[...] = early_halo_ref[...]
+
+    @pl.when(jnp.logical_not(waits_long()))
+    def _():
+        find_field(last, begin_ref, innov_ref, obs_ref, own_ref, halo_ref, *scratch)
+
+
+HBM = pl.BlockSpec(memory_space=pltpu.HBM)
+FIELD = (jax.ShapeDtypeStruct((OWN_TILES, LANES), jnp.float32), jax.ShapeDtypeStruct((1, LANES), jnp.float32))
+
+
+def field_scratch():
+    return [
+        pltpu.SMEM((BLK_DEV,), jnp.int32),
+        pltpu.SMEM((BLK_DEV + GROUP,), jnp.int32),
+        pltpu.VMEM((BLK_DEV, LANES), jnp.float32),
+        pltpu.VMEM((BLK_DEV, TILE, TILE), jnp.bfloat16),
+        pltpu.VMEM((2 * SUBLANES, LANES), jnp.float32),
+        pltpu.VMEM((1, LANES), jnp.float32),
+        pltpu.SemaphoreType.DMA,
+        pltpu.SemaphoreType.DMA,
+        pltpu.SemaphoreType.DMA((BLK_DEV // PIECE,)),
+    ]
+
+
+def in_hbm(*operands):
+    return [pltpu.with_memory_space_constraint(x, pltpu.HBM) for x in operands]
+
+
+def early(modes, tile_start, innovations, obs_weights, last):
     return pl.pallas_call(
-        lay_kernel,
-        out_shape=jax.ShapeDtypeStruct(modes.shape, modes.dtype),
-        in_specs=[pl.BlockSpec(memory_space=pltpu.HBM)],
-        out_specs=VMEM,
-        scratch_shapes=[pltpu.SemaphoreType.DMA((4,))],
+        functools.partial(early_kernel, last),
+        out_shape=(jax.ShapeDtypeStruct(modes.shape, modes.dtype),) + FIELD,
+        in_specs=[HBM] * 4,
+        out_specs=(VMEM,) * 3,
+        scratch_shapes=[pltpu.SemaphoreType.DMA((4,))] + field_scratch(),
         compiler_params=SMALL,
-        name="lay",
-    )(pltpu.with_memory_space_constraint(modes, pltpu.HBM))
+        name="early",
+    )(*in_hbm(modes, tile_start, innovations, obs_weights))
+
+
+def late(tile_start, innovations, obs_weights, own, halo, last):
+    return pl.pallas_call(
+        functools.partial(late_kernel, last),
+        out_shape=FIELD,
+        in_specs=[HBM] * 3 + [VMEM] * 2,
+        out_specs=(VMEM,) * 2,
+        scratch_shapes=field_scratch(),
+        compiler_params=SMALL,
+        cost_estimate=pl.CostEstimate(flops=2**22, bytes_accessed=2**22, transcendentals=0),
+        name="late",
+    )(*in_hbm(tile_start, innovations, obs_weights), own, halo)
 
 
 def project_kernel(last, own_ref, halo_ref, members_ref, modes_ref, out_ref):
@@ -254,11 +282,11 @@
     mode_count = lax.axis_size(MODE)
     space_count = lax.axis_size(SPACE)
     last = mode_count - 1
-    laid = lay(modes)
+    laid, own, halo = early(modes, tile_start, innovations, obs_weights, last)
     all_modes = lax.all_to_all(
         laid, MODE, split_axis=1, concat_axis=0, axis_index_groups=places(MODE), tiled=True
     )
-    own, halo = field(tile_start, innovations, obs_weights, last)
+    own, halo = late(tile_start, innovations, obs_weights, own, halo, last)
     route = []
     for s in range(space_count):
         behind, ahead = (s - 1) % space_count, (s + 1) % space_count

time: 63.7 us -> 63.2 us (level)
  waiting for transfers between devices: 3.88 us -> 6.24 us
  blocking collectives: 35.2 us -> 33.8 us
  starting transfers between devices: 18.1 us -> 17.2 us
  Pallas kernels: 5.32 us -> 4.62 us
    all_to_all x1, waiting for transfers between devices: 3.87 us -> 6.24 us  [on_device(): lax.all_to_all(laid, MODE, split_axis=1, concat_axis=0, axis_index_groups...]
    all_to_all x3, blocking collectives: 35.2 us -> 33.8 us  [exchange(): lax.all_to_all(x, axis, split_axis=0, concat_axis=0, axis_index_groups=pl...]
    all_to_all x1, starting transfers between devices: 17.4 us -> 16.6 us  [on_device(): lax.all_to_all(laid, MODE, split_axis=1, concat_axis=0, axis_index_groups...]
    pallas_call x2, Pallas kernels: 4.18 us -> 3.48 us  [the longest x1 3.37 us: early(): pl.pallas_call(functools.partial(early_kernel, last), out_shape=(jax.Shap...]
  transfers between devices with their start and end apart: 2 -> 2, of which waited for: 1 -> 1; matrix products, arithmetic and copies ran while one was open for 0% -> 0% of each run, Pallas kernels for 4% -> 0%
where the time goes in v1:
time: 63.2 us; the launch traced here: 62.9 us
  blocking collectives  33.8 us (53%)
  starting transfers between devices  17.2 us (27%)
  waiting for transfers between devices  6.24 us (10%)
  Pallas kernels  4.62 us (7%)
  between operations  0.71 us (1%)
    all_to_all x3, blocking collectives, exchange(): lax.all_to_all(x, axis, split_axis=0, concat_axis=0, axis_index_groups=pl...  33.8 us
    all_to_all x1, starting transfers between devices, on_device(): lax.all_to_all(laid, MODE, split_axis=1, concat_axis=0, axis_index_groups...  16.6 us
    all_to_all x1, waiting for transfers between devices, on_device(): lax.all_to_all(laid, MODE, split_axis=1, concat_axis=0, axis_index_groups...  6.24 us
    pallas_call x1, Pallas kernels, early(): pl.pallas_call(functools.partial(early_kernel, last), out_shape=(jax.Shap...  3.37 us
  transfers between devices with their start and end apart: 2, of which 1 were waited for; matrix products, arithmetic and copies ran while one was open for 0% of the time, Pallas kernels for 0%

profile of v1, /device:TPU:1, one launch (start us, length us, event | category | flops | bytes accessed | tf_op | source)
XLA Modules:
  0.0 62.9 jit_solution(4186770665139677333)
XLA Ops:
  0.6 0.0 copy-start
  0.6 3.4 %early.1 = (bf16[4,32768]{1,0:T(4,128)(2,1)}, f32[8,128]{1,0:T(8,128)S(1)}, f32[1,128]{1,0:T(1,128)S(1)}) custom-call(bf16[4,32768]{1,0:T(4,128)(2,1)} %modes_ref.1, s32[128]{0:T(128)} %begin_ref.3, f32[128,128]{1,0:T(8,128)} %innov_ref.3, bf16[128,128,128]{2,1,0:T(8,128)(2,1)} %obs_ref.3), custom_call_target="tpu_custom_call" | custom-call | tf_op jit(solution)/shard_map/early/pallas_call | solution.py:171
  4.0 16.6 %all-to-all-start = ((bf16[4,32,1024]{2,0,1:T(4,128)(2,1)}), bf16[4,32,1024]{2,0,1:T(4,128)(2,1)S(1)}, u32[]{:S(2)}, u32[]{:S(2)}) async-start(bf16[4,32,1024]{2,0,1:T(4,128)(2,1)} %bitcast), calls=%async_computation | async-start | bytes 524288 | tf_op jit(solution)/shard_map/all_to_all | solution.py:286
  20.6 0.1 late.1
  20.7 0.7 %collective-permute-start = (f32[1,128]{1,0:T(1,128)S(1)}, f32[1,128]{1,0:T(1,128)S(1)}, u32[]{:S(2)}, u32[]{:S(2)}) collective-permute-start(f32[1,128]{1,0:T(1,128)S(1)} %get-tuple-element.12), channel_id=1, source_target_pairs={{0,32},{31,511},{32,64},{63,31},{64,96},{95,63},{96,128},{127,95},... | collective-permute-start | bytes 1544 | tf_op jit(solution)/shard_map/ppermute | solution.py:295
  21.4 6.2 %all-to-all-done = bf16[4,32,1024]{2,0,1:T(4,128)(2,1)S(1)} async-done(((bf16[4,32,1024]{2,0,1:T(4,128)(2,1)}), bf16[4,32,1024]{2,0,1:T(4,128)(2,1)S(1)}, u32[]{:S(2)}, u32[]{:S(2)}) %all-to-all-start) | async-done | bytes 262176 | tf_op jit(solution)/shard_map/all_to_all | solution.py:286
  27.6 0.1 all_to_all.26.modes_ref
  27.7 0.0 collective-permute-done.halo_ref
  27.7 0.0 copy-done
  27.7 0.3 project.1
  28.0 8.5 %all_to_all.34 = f32[16,1,640]{2,1,0:T(1,128)S(1)} all-to-all(f32[16,1,640]{2,1,0:T(1,128)S(1)} %bitcast.7), channel_id=1, replica_groups={{18,19,16,17,2,3,0,1,50,51,48,49,34,35,32,33},{22,23,20,21,6,7,4,5,54,5..., dimensions={0} | all-to-all | bytes 81920 | tf_op jit(solution)/shard_map/all_to_all | solution.py:274
  36.7 15.6 %all_to_all.35 = f32[32,1,640]{2,1,0:T(1,128)S(1)} all-to-all(f32[32,1,640]{2,1,0:T(1,128)S(1)} %broadcast_in_dim.4), channel_id=1, replica_groups={{264,268,256,260,328,332,320,324,392,396,384,388,456,460,448,452,8,12,0..., dimensions={0} | all-to-all | bytes 163840 | tf_op jit(solution)/shard_map/all_to_all | solution.py:274
  52.3 0.1 reduce_sum.19
  52.4 9.6 %all_to_all.36 = f32[16,1,640]{2,1,0:T(1,128)S(1)} all-to-all(f32[16,1,640]{2,1,0:T(1,128)S(1)} %broadcast_in_dim.5), channel_id=1, replica_groups={{18,19,16,17,2,3,0,1,50,51,48,49,34,35,32,33},{22,23,20,21,6,7,4,5,54,5..., dimensions={0} | all-to-all | bytes 81920 | tf_op jit(solution)/shard_map/all_to_all | solution.py:274
  62.0 0.8 %finish.1 = (f32[8,128]{1,0:T(8,128)}, f32[4,80]{1,0:T(4,128)}) custom-call(f32[80,128]{1,0:T(8,128)S(1)} %bitcast.6, bf16[80,1024]{1,0:T(8,128)(2,1)S(1)} %copy-done, bf16[128,1024]{1,0:T(8,128)(2,1)S(1)} %all_to_all.26.modes_ref), custom_call_target="tpu_custom_call" | custom-call | tf_op jit(solution)/shard_map/finish/pallas_call | solution.py:243
  (3 shorter events, 0.1 us)
Async XLA Ops:
  0.6 27.1 %copy-start = (bf16[80,1024]{1,0:T(8,128)(2,1)S(1)}, bf16[80,1024]{1,0:T(8,128)(2,1)}, u32[]{:S(2)}) copy-start(bf16[80,1024]{1,0:T(8,128)(2,1)} %members_ref.3) | copy-start | bytes 491524
  4.0 23.6 %all-to-all-start = ((bf16[4,32,1024]{2,0,1:T(4,128)(2,1)}), bf16[4,32,1024]{2,0,1:T(4,128)(2,1)S(1)}, u32[]{:S(2)}, u32[]{:S(2)}) async-start(bf16[4,32,1024]{2,0,1:T(4,128)(2,1)} %bitcast), calls=%async_computation | async-start | bytes 524288 | tf_op jit(solution)/shard_map/all_to_all | solution.py:286
  20.7 7.0 %collective-permute-start = (f32[1,128]{1,0:T(1,128)S(1)}, f32[1,128]{1,0:T(1,128)S(1)}, u32[]{:S(2)}, u32[]{:S(2)}) collective-permute-start(f32[1,128]{1,0:T(1,128)S(1)} %get-tuple-element.12), channel_id=1, source_target_pairs={{0,32},{31,511},{32,64},{63,31},{64,96},{95,63},{96,128},{127,95},... | collective-permute-start | bytes 1544 | tf_op jit(solution)/shard_map/ppermute | solution.py:295

commit v2 on v1

--- a/solution.py
+++ b/solution.py
@@ -270,8 +270,17 @@
     return at
 
 
+def far_groups():
+    sizes = [lax.axis_size(a) for a in FAR]
+    order = np.array(places(FAR)).reshape(sizes)
+    cores = lax.axis_size("core")
+    return [[int(p) * cores + c for p in (order.T if c else order).reshape(-1)] for c in range(cores)]
+
+
 def exchange(x, axis):
-    return lax.all_to_all(x, axis, split_axis=0, concat_axis=0, axis_index_groups=places(axis), tiled=True)
+    groups = far_groups() if axis == FAR else places(axis)
+    axis = FAR + ("core",) if axis == FAR else axis
+    return lax.all_to_all(x, axis, split_axis=0, concat_axis=0, axis_index_groups=groups, tiled=True)
 
 
 def everywhere(x, axis):

time: 63.2 us -> 63.2 us (level)
  no operation moved by 1% of the time
where the time goes in v2:
time: 63.2 us; the launch traced here: 62.9 us
  blocking collectives  33.6 us (53%)
  starting transfers between devices  17.5 us (28%)
  waiting for transfers between devices  6.24 us (10%)
  Pallas kernels  4.63 us (7%)
  between operations  0.71 us (1%)
    all_to_all x3, blocking collectives, exchange(): lax.all_to_all(x, axis, split_axis=0, concat_axis=0, axis_index_groups=gr...  33.6 us
    all_to_all x1, starting transfers between devices, on_device(): lax.all_to_all(laid, MODE, split_axis=1, concat_axis=0, axis_index_groups...  16.8 us
    all_to_all x1, waiting for transfers between devices, on_device(): lax.all_to_all(laid, MODE, split_axis=1, concat_axis=0, axis_index_groups...  6.24 us
    pallas_call x1, Pallas kernels, early(): pl.pallas_call(functools.partial(early_kernel, last), out_shape=(jax.Shap...  3.38 us
  transfers between devices with their start and end apart: 2, of which 1 were waited for; matrix products, arithmetic and copies ran while one was open for 0% of the time, Pallas kernels for 0%

profile of v2, /device:TPU:1, one launch (start us, length us, event | category | flops | bytes accessed | tf_op | source)
XLA Modules:
  0.0 62.9 jit_solution(14766153560301357579)
XLA Ops:
  0.6 0.0 copy-start
  0.6 3.4 %early.1 = (bf16[4,32768]{1,0:T(4,128)(2,1)}, f32[8,128]{1,0:T(8,128)S(1)}, f32[1,128]{1,0:T(1,128)S(1)}) custom-call(bf16[4,32768]{1,0:T(4,128)(2,1)} %modes_ref.1, s32[128]{0:T(128)} %begin_ref.3, f32[128,128]{1,0:T(8,128)} %innov_ref.3, bf16[128,128,128]{2,1,0:T(8,128)(2,1)} %obs_ref.3), custom_call_target="tpu_custom_call" | custom-call | tf_op jit(solution)/shard_map/early/pallas_call | solution.py:171
  4.0 16.8 %all-to-all-start = ((bf16[4,32,1024]{2,0,1:T(4,128)(2,1)}), bf16[4,32,1024]{2,0,1:T(4,128)(2,1)S(1)}, u32[]{:S(2)}, u32[]{:S(2)}) async-start(bf16[4,32,1024]{2,0,1:T(4,128)(2,1)} %bitcast), calls=%async_computation | async-start | bytes 524288 | tf_op jit(solution)/shard_map/all_to_all | solution.py:295
  20.8 0.1 late.1
  21.0 0.7 %collective-permute-start = (f32[1,128]{1,0:T(1,128)S(1)}, f32[1,128]{1,0:T(1,128)S(1)}, u32[]{:S(2)}, u32[]{:S(2)}) collective-permute-start(f32[1,128]{1,0:T(1,128)S(1)} %get-tuple-element.12), channel_id=1, source_target_pairs={{0,32},{31,511},{32,64},{63,31},{64,96},{95,63},{96,128},{127,95},... | collective-permute-start | bytes 1544 | tf_op jit(solution)/shard_map/ppermute | solution.py:304
  21.6 6.2 %all-to-all-done = bf16[4,32,1024]{2,0,1:T(4,128)(2,1)S(1)} async-done(((bf16[4,32,1024]{2,0,1:T(4,128)(2,1)}), bf16[4,32,1024]{2,0,1:T(4,128)(2,1)S(1)}, u32[]{:S(2)}, u32[]{:S(2)}) %all-to-all-start) | async-done | bytes 262176 | tf_op jit(solution)/shard_map/all_to_all | solution.py:295
  27.9 0.1 all_to_all.26.modes_ref
  27.9 0.0 collective-permute-done.halo_ref
  27.9 0.0 copy-done
  28.0 0.3 project.1
  28.3 8.5 %all_to_all.34 = f32[16,1,640]{2,1,0:T(1,128)S(1)} all-to-all(f32[16,1,640]{2,1,0:T(1,128)S(1)} %bitcast.7), channel_id=1, replica_groups={{18,19,16,17,2,3,0,1,50,51,48,49,34,35,32,33},{22,23,20,21,6,7,4,5,54,5..., dimensions={0} | all-to-all | bytes 81920 | tf_op jit(solution)/shard_map/all_to_all | solution.py:283
  36.9 15.5 %all_to_all.35 = f32[32,1,640]{2,1,0:T(1,128)S(1)} all-to-all(f32[32,1,640]{2,1,0:T(1,128)S(1)} %broadcast_in_dim.4), channel_id=1, replica_groups={{264,268,256,260,328,332,320,324,392,396,384,388,456,460,448,452,8,12,0..., dimensions={0} | all-to-all | bytes 163840 | tf_op jit(solution)/shard_map/all_to_all | solution.py:283
  52.4 0.1 reduce_sum.19
  52.5 9.6 %all_to_all.36 = f32[16,1,640]{2,1,0:T(1,128)S(1)} all-to-all(f32[16,1,640]{2,1,0:T(1,128)S(1)} %broadcast_in_dim.5), channel_id=1, replica_groups={{18,19,16,17,2,3,0,1,50,51,48,49,34,35,32,33},{22,23,20,21,6,7,4,5,54,5..., dimensions={0} | all-to-all | bytes 81920 | tf_op jit(solution)/shard_map/all_to_all | solution.py:283
  62.1 0.8 %finish.1 = (f32[8,128]{1,0:T(8,128)}, f32[4,80]{1,0:T(4,128)}) custom-call(f32[80,128]{1,0:T(8,128)S(1)} %bitcast.6, bf16[80,1024]{1,0:T(8,128)(2,1)S(1)} %copy-done, bf16[128,1024]{1,0:T(8,128)(2,1)S(1)} %all_to_all.26.modes_ref), custom_call_target="tpu_custom_call" | custom-call | tf_op jit(solution)/shard_map/finish/pallas_call | solution.py:243
  (3 shorter events, 0.1 us)
Async XLA Ops:
  0.6 27.3 %copy-start = (bf16[80,1024]{1,0:T(8,128)(2,1)S(1)}, bf16[80,1024]{1,0:T(8,128)(2,1)}, u32[]{:S(2)}) copy-start(bf16[80,1024]{1,0:T(8,128)(2,1)} %members_ref.3) | copy-start | bytes 491524
  4.0 23.8 %all-to-all-start = ((bf16[4,32,1024]{2,0,1:T(4,128)(2,1)}), bf16[4,32,1024]{2,0,1:T(4,128)(2,1)S(1)}, u32[]{:S(2)}, u32[]{:S(2)}) async-start(bf16[4,32,1024]{2,0,1:T(4,128)(2,1)} %bitcast), calls=%async_computation | async-start | bytes 524288 | tf_op jit(solution)/shard_map/all_to_all | solution.py:295
  21.0 7.0 %collective-permute-start = (f32[1,128]{1,0:T(1,128)S(1)}, f32[1,128]{1,0:T(1,128)S(1)}, u32[]{:S(2)}, u32[]{:S(2)}) collective-permute-start(f32[1,128]{1,0:T(1,128)S(1)} %get-tuple-element.12), channel_id=1, source_target_pairs={{0,32},{31,511},{32,64},{63,31},{64,96},{95,63},{96,128},{127,95},... | collective-permute-start | bytes 1544 | tf_op jit(solution)/shard_map/ppermute | solution.py:304

commit v3 on v1

--- a/solution.py
+++ b/solution.py
@@ -21,6 +21,7 @@
 SUBLANES = 8
 GROUP = 4
 PIECE = 16
+PIECES = 8
 VMEM = pl.BlockSpec(memory_space=pltpu.VMEM)
 SMALL = pltpu.CompilerParams(vmem_limit_bytes=12 * 2**20)
 MODE = ("xhi", "zhi", "zlo", "core")
@@ -116,13 +117,13 @@
 
 
 def early_kernel(last, modes_ref, begin_ref, innov_ref, obs_ref, laid_ref, own_ref, halo_ref, lay_sems, *scratch):
-    part = modes_ref.shape[1] // 4
-    copies = [
-        pltpu.make_async_copy(
-            modes_ref.at[:, pl.ds(q * part, part)], laid_ref.at[:, pl.ds((3 - q) * part, part)], lay_sems.at[q]
+    part = modes_ref.shape[0] // PIECES
+    copies = []
+    for q in range(PIECES):
+        to = (3 - 4 * q // PIECES) * (PIECES // 4) + q % (PIECES // 4)
+        copies.append(
+            pltpu.make_async_copy(modes_ref.at[pl.ds(q * part, part)], laid_ref.at[pl.ds(to * part, part)], lay_sems.at[q])
         )
-        for q in range(4)
-    ]
     for copy in copies:
         copy.start()
 
@@ -173,7 +174,7 @@
         out_shape=(jax.ShapeDtypeStruct(modes.shape, modes.dtype),) + FIELD,
         in_specs=[HBM] * 4,
         out_specs=(VMEM,) * 3,
-        scratch_shapes=[pltpu.SemaphoreType.DMA((4,))] + field_scratch(),
+        scratch_shapes=[pltpu.SemaphoreType.DMA((PIECES,))] + field_scratch(),
         compiler_params=SMALL,
         name="early",
     )(*in_hbm(modes, tile_start, innovations, obs_weights))
@@ -282,7 +283,9 @@
     mode_count = lax.axis_size(MODE)
     space_count = lax.axis_size(SPACE)
     last = mode_count - 1
-    laid, own, halo = early(modes, tile_start, innovations, obs_weights, last)
+    columns = modes.reshape(MODE_DEV, -1, LANES).transpose(1, 0, 2)
+    laid, own, halo = early(columns, tile_start, innovations, obs_weights, last)
+    laid = laid.transpose(1, 0, 2).reshape(modes.shape)
     all_modes = lax.all_to_all(
         laid, MODE, split_axis=1, concat_axis=0, axis_index_groups=places(MODE), tiled=True
     )

time: 63.2 us -> 63.2 us (level)
  no operation moved by 1% of the time
where the time goes in v3:
time: 63.2 us; the launch traced here: 62.8 us
  blocking collectives  33.5 us (53%)
  starting transfers between devices  17.2 us (27%)
  waiting for transfers between devices  6.24 us (10%)
  Pallas kernels  4.9 us (8%)
  between operations  0.71 us (1%)
    all_to_all x3, blocking collectives, exchange(): lax.all_to_all(x, axis, split_axis=0, concat_axis=0, axis_index_groups=pl...  33.5 us
    all_to_all x1, starting transfers between devices, on_device(): lax.all_to_all(laid, MODE, split_axis=1, concat_axis=0, axis_index_groups...  16.6 us
    all_to_all x1, waiting for transfers between devices, on_device(): lax.all_to_all(laid, MODE, split_axis=1, concat_axis=0, axis_index_groups...  6.24 us
    pallas_call x1, Pallas kernels, early(): pl.pallas_call(functools.partial(early_kernel, last), out_shape=(jax.Shap...  3.65 us
  transfers between devices with their start and end apart: 2, of which 1 were waited for; matrix products, arithmetic and copies ran while one was open for 0% of the time, Pallas kernels for 0%

profile of v3, /device:TPU:1, one launch (start us, length us, event | category | flops | bytes accessed | tf_op | source)
XLA Modules:
  0.0 62.8 jit_solution(16494480389939806026)
XLA Ops:
  0.6 0.0 copy-start
  0.6 3.7 %early.1 = (bf16[256,4,128]{2,1,0:T(4,128)(2,1)}, f32[8,128]{1,0:T(8,128)S(1)}, f32[1,128]{1,0:T(1,128)S(1)}) custom-call(bf16[256,4,128]{2,1,0:T(4,128)(2,1)} %bitcast.14, s32[128]{0:T(128)} %begin_ref.3, f32[128,128]{1,0:T(8,128)} %innov_ref.3, bf16[128,128,128]{2,1,0:T(8,128)(2,1)} %obs_ref.3), custom_call_target="tpu_custom_call" | custom-call | tf_op jit(solution)/shard_map/early/pallas_call | solution.py:172
  4.3 16.6 %all-to-all-start = ((bf16[4,32,1024]{2,0,1:T(4,128)(2,1)}), bf16[4,32,1024]{2,0,1:T(4,128)(2,1)S(1)}, u32[]{:S(2)}, u32[]{:S(2)}) async-start(bf16[4,32,1024]{2,0,1:T(4,128)(2,1)} %bitcast.3), calls=%async_computation | async-start | bytes 524288 | tf_op jit(solution)/shard_map/all_to_all | solution.py:289
  20.9 0.1 late.1
  21.0 0.7 %collective-permute-start = (f32[1,128]{1,0:T(1,128)S(1)}, f32[1,128]{1,0:T(1,128)S(1)}, u32[]{:S(2)}, u32[]{:S(2)}) collective-permute-start(f32[1,128]{1,0:T(1,128)S(1)} %get-tuple-element.12), channel_id=1, source_target_pairs={{0,32},{31,511},{32,64},{63,31},{64,96},{95,63},{96,128},{127,95},... | collective-permute-start | bytes 1544 | tf_op jit(solution)/shard_map/ppermute | solution.py:298
  21.7 6.2 %all-to-all-done = bf16[4,32,1024]{2,0,1:T(4,128)(2,1)S(1)} async-done(((bf16[4,32,1024]{2,0,1:T(4,128)(2,1)}), bf16[4,32,1024]{2,0,1:T(4,128)(2,1)S(1)}, u32[]{:S(2)}, u32[]{:S(2)}) %all-to-all-start) | async-done | bytes 262176 | tf_op jit(solution)/shard_map/all_to_all | solution.py:289
  27.9 0.1 all_to_all.26.modes_ref
  28.0 0.0 collective-permute-done.halo_ref
  28.0 0.0 copy-done
  28.0 0.3 project.1
  28.3 8.5 %all_to_all.34 = f32[16,1,640]{2,1,0:T(1,128)S(1)} all-to-all(f32[16,1,640]{2,1,0:T(1,128)S(1)} %bitcast.12), channel_id=1, replica_groups={{18,19,16,17,2,3,0,1,50,51,48,49,34,35,32,33},{22,23,20,21,6,7,4,5,54,5..., dimensions={0} | all-to-all | bytes 81920 | tf_op jit(solution)/shard_map/all_to_all | solution.py:275
  36.9 15.3 %all_to_all.35 = f32[32,1,640]{2,1,0:T(1,128)S(1)} all-to-all(f32[32,1,640]{2,1,0:T(1,128)S(1)} %broadcast_in_dim.4), channel_id=1, replica_groups={{264,268,256,260,328,332,320,324,392,396,384,388,456,460,448,452,8,12,0..., dimensions={0} | all-to-all | bytes 163840 | tf_op jit(solution)/shard_map/all_to_all | solution.py:275
  52.3 0.1 reduce_sum.19
  52.4 9.6 %all_to_all.36 = f32[16,1,640]{2,1,0:T(1,128)S(1)} all-to-all(f32[16,1,640]{2,1,0:T(1,128)S(1)} %broadcast_in_dim.5), channel_id=1, replica_groups={{18,19,16,17,2,3,0,1,50,51,48,49,34,35,32,33},{22,23,20,21,6,7,4,5,54,5..., dimensions={0} | all-to-all | bytes 81920 | tf_op jit(solution)/shard_map/all_to_all | solution.py:275
  62.0 0.8 %finish.1 = (f32[8,128]{1,0:T(8,128)}, f32[4,80]{1,0:T(4,128)}) custom-call(f32[80,128]{1,0:T(8,128)S(1)} %bitcast.11, bf16[80,1024]{1,0:T(8,128)(2,1)S(1)} %copy-done, bf16[128,1024]{1,0:T(8,128)(2,1)S(1)} %all_to_all.26.modes_ref), custom_call_target="tpu_custom_call" | custom-call | tf_op jit(solution)/shard_map/finish/pallas_call | solution.py:244
  (3 shorter events, 0.1 us)
Async XLA Ops:
  0.6 27.4 %copy-start = (bf16[80,1024]{1,0:T(8,128)(2,1)S(1)}, bf16[80,1024]{1,0:T(8,128)(2,1)}, u32[]{:S(2)}) copy-start(bf16[80,1024]{1,0:T(8,128)(2,1)} %members_ref.3) | copy-start | bytes 491524
  4.3 23.6 %all-to-all-start = ((bf16[4,32,1024]{2,0,1:T(4,128)(2,1)}), bf16[4,32,1024]{2,0,1:T(4,128)(2,1)S(1)}, u32[]{:S(2)}, u32[]{:S(2)}) async-start(bf16[4,32,1024]{2,0,1:T(4,128)(2,1)} %bitcast.3), calls=%async_computation | async-start | bytes 524288 | tf_op jit(solution)/shard_map/all_to_all | solution.py:289
  21.0 7.0 %collective-permute-start = (f32[1,128]{1,0:T(1,128)S(1)}, f32[1,128]{1,0:T(1,128)S(1)}, u32[]{:S(2)}, u32[]{:S(2)}) collective-permute-start(f32[1,128]{1,0:T(1,128)S(1)} %get-tuple-element.12), channel_id=1, source_target_pairs={{0,32},{31,511},{32,64},{63,31},{64,96},{95,63},{96,128},{127,95},... | collective-permute-start | bytes 1544 | tf_op jit(solution)/shard_map/ppermute | solution.py:298

commit v4 on v1

--- a/solution.py
+++ b/solution.py
@@ -115,23 +115,10 @@
     return lax.axis_index("zhi") < lax.axis_size("zhi") // 2
 
 
-def early_kernel(last, modes_ref, begin_ref, innov_ref, obs_ref, laid_ref, own_ref, halo_ref, lay_sems, *scratch):
-    part = modes_ref.shape[1] // 4
-    copies = [
-        pltpu.make_async_copy(
-            modes_ref.at[:, pl.ds(q * part, part)], laid_ref.at[:, pl.ds((3 - q) * part, part)], lay_sems.at[q]
-        )
-        for q in range(4)
-    ]
-    for copy in copies:
-        copy.start()
-
+def early_kernel(last, begin_ref, innov_ref, obs_ref, own_ref, halo_ref, *scratch):
     @pl.when(waits_long())
     def _():
         find_field(last, begin_ref, innov_ref, obs_ref, own_ref, halo_ref, *scratch)
-
-    for copy in copies:
-        copy.wait()
 
 
 def late_kernel(last, begin_ref, innov_ref, obs_ref, early_own_ref, early_halo_ref, own_ref, halo_ref, *scratch):
@@ -167,16 +154,16 @@
     return [pltpu.with_memory_space_constraint(x, pltpu.HBM) for x in operands]
 
 
-def early(modes, tile_start, innovations, obs_weights, last):
+def early(tile_start, innovations, obs_weights, last):
     return pl.pallas_call(
         functools.partial(early_kernel, last),
-        out_shape=(jax.ShapeDtypeStruct(modes.shape, modes.dtype),) + FIELD,
-        in_specs=[HBM] * 4,
-        out_specs=(VMEM,) * 3,
-        scratch_shapes=[pltpu.SemaphoreType.DMA((4,))] + field_scratch(),
+        out_shape=FIELD,
+        in_specs=[HBM] * 3,
+        out_specs=(VMEM,) * 2,
+        scratch_shapes=field_scratch(),
         compiler_params=SMALL,
         name="early",
-    )(*in_hbm(modes, tile_start, innovations, obs_weights))
+    )(*in_hbm(tile_start, innovations, obs_weights))
 
 
 def late(tile_start, innovations, obs_weights, own, halo, last):
@@ -282,7 +269,9 @@
     mode_count = lax.axis_size(MODE)
     space_count = lax.axis_size(SPACE)
     last = mode_count - 1
-    laid, own, halo = early(modes, tile_start, innovations, obs_weights, last)
+    own, halo = early(tile_start, innovations, obs_weights, last)
+    laid = jnp.concatenate(jnp.split(modes, 4, axis=1)[::-1], axis=1)
+    laid, own, halo = lax.optimization_barrier((laid, own, halo))
     all_modes = lax.all_to_all(
         laid, MODE, split_axis=1, concat_axis=0, axis_index_groups=places(MODE), tiled=True
     )

time: 63.2 us -> 63.4 us (level)
  local copies, waits for them, and re-layouts: 0.14 us -> 1.17 us
  other arithmetic: 0.11 us -> 0.91 us
  blocking collectives: 33.8 us -> 33 us
    split x0 -> x1, local copies, waits for them, and re-layouts: none -> 1.03 us  [on_device(): laid = jnp.concatenate(jnp.split(modes, 4, axis=1)[::-1], axis=1)]
    all_to_all x3, blocking collectives: 33.8 us -> 33 us  [exchange(): lax.all_to_all(x, axis, split_axis=0, concat_axis=0, axis_index_groups=pl...]
    concatenate x0 -> x1, other arithmetic: none -> 0.81 us  [on_device(): laid = jnp.concatenate(jnp.split(modes, 4, axis=1)[::-1], axis=1)]
where the time goes in v4:
time: 63.4 us; the launch traced here: 63 us
  blocking collectives  33 us (52%)
  starting transfers between devices  17 us (27%)
  waiting for transfers between devices  6.24 us (10%)
  Pallas kernels  3.99 us (6%)
  local copies, waits for them, and re-layouts  1.17 us (2%)
  other arithmetic  0.91 us (1%)
  between operations  0.72 us (1%)
    all_to_all x3, blocking collectives, exchange(): lax.all_to_all(x, axis, split_axis=0, concat_axis=0, axis_index_groups=pl...  33 us
    all_to_all x1, starting transfers between devices, on_device(): lax.all_to_all(laid, MODE, split_axis=1, concat_axis=0, axis_index_groups...  16.4 us
    all_to_all x1, waiting for transfers between devices, on_device(): lax.all_to_all(laid, MODE, split_axis=1, concat_axis=0, axis_index_groups...  6.24 us
    pallas_call x1, Pallas kernels, early(): pl.pallas_call(functools.partial(early_kernel, last), out_shape=FIELD, in...  2.73 us
  transfers between devices with their start and end apart: 2, of which 1 were waited for; matrix products, arithmetic and copies ran while one was open for 0% of the time, Pallas kernels for 0%

profile of v4, /device:TPU:1, one launch (start us, length us, event | category | flops | bytes accessed | tf_op | source)
XLA Modules:
  0.0 63.0 jit_solution(3599290481884694734)
XLA Ops:
  0.6 1.0 %fusion = (bf16[4,8192]{1,0:T(4,128)(2,1)S(1)}, bf16[4,8192]{1,0:T(4,128)(2,1)S(1)}, bf16[4,8192]{1,0:T(4,128)(2,1)S(1)}, bf16[4,8192]{1,0:T(4,128)(2,1)S(1)}) fusion(bf16[4,32768]{1,0:T(4,128)(2,1)} %param.6), kind=kLoop, calls=%fused_computation.1 | loop fusion | bytes 524288 | tf_op jit(solution)/shard_map/split | solution.py:273
  1.7 0.0 copy-start
  1.7 2.7 %early.1 = (f32[8,128]{1,0:T(8,128)S(1)}, f32[1,128]{1,0:T(1,128)S(1)}) custom-call(s32[128]{0:T(128)} %begin_ref.3, f32[128,128]{1,0:T(8,128)} %innov_ref.3, bf16[128,128,128]{2,1,0:T(8,128)(2,1)} %obs_ref.3), custom_call_target="tpu_custom_call" | custom-call | tf_op jit(solution)/shard_map/early/pallas_call | solution.py:158
  4.4 0.8 %pad_maximum_fusion = bf16[4,32768]{1,0:T(4,128)(2,1)} fusion(bf16[4,8192]{1,0:T(4,128)(2,1)S(1)} %get-tuple-element.22, bf16[4,8192]{1,0:T(4,128)(2,1)S(1)} %get-tuple-element.23, bf16[4,8192]{1,0:T(4,128)(2,1)S(1)} %get-tuple-element.21, bf16[4,8192]{1,0:T(4,128)(2,1)S(1)} %get-tuple-element.20), kind=kLoop, calls=%fused_computation | loop fusion | flops 1048576 | bytes 524288 | tf_op jit(solution)/shard_map/concatenate | solution.py:273
  5.2 16.4 %all-to-all-start = ((bf16[4,32,1024]{2,0,1:T(4,128)(2,1)}), bf16[4,32,1024]{2,0,1:T(4,128)(2,1)S(1)}, u32[]{:S(2)}, u32[]{:S(2)}) async-start(bf16[4,32,1024]{2,0,1:T(4,128)(2,1)} %bitcast), calls=%async_computation | async-start | bytes 524288 | tf_op jit(solution)/shard_map/all_to_all | solution.py:275
  21.6 0.1 late.1
  21.7 0.7 %collective-permute-start = (f32[1,128]{1,0:T(1,128)S(1)}, f32[1,128]{1,0:T(1,128)S(1)}, u32[]{:S(2)}, u32[]{:S(2)}) collective-permute-start(f32[1,128]{1,0:T(1,128)S(1)} %get-tuple-element.16), channel_id=1, source_target_pairs={{0,32},{31,511},{32,64},{63,31},{64,96},{95,63},{96,128},{127,95},... | collective-permute-start | bytes 1544 | tf_op jit(solution)/shard_map/ppermute | solution.py:284
  22.4 6.2 %all-to-all-done = bf16[4,32,1024]{2,0,1:T(4,128)(2,1)S(1)} async-done(((bf16[4,32,1024]{2,0,1:T(4,128)(2,1)}), bf16[4,32,1024]{2,0,1:T(4,128)(2,1)S(1)}, u32[]{:S(2)}, u32[]{:S(2)}) %all-to-all-start) | async-done | bytes 262176 | tf_op jit(solution)/shard_map/all_to_all | solution.py:275
  28.6 0.1 all_to_all.26.modes_ref
  28.7 0.0 collective-permute-done.halo_ref
  28.7 0.0 copy-done
  28.7 0.3 project.1
  29.0 8.5 %all_to_all.34 = f32[16,1,640]{2,1,0:T(1,128)S(1)} all-to-all(f32[16,1,640]{2,1,0:T(1,128)S(1)} %bitcast.7), channel_id=1, replica_groups={{18,19,16,17,2,3,0,1,50,51,48,49,34,35,32,33},{22,23,20,21,6,7,4,5,54,5..., dimensions={0} | all-to-all | bytes 81920 | tf_op jit(solution)/shard_map/all_to_all | solution.py:261
  37.6 14.8 %all_to_all.35 = f32[32,1,640]{2,1,0:T(1,128)S(1)} all-to-all(f32[32,1,640]{2,1,0:T(1,128)S(1)} %broadcast_in_dim.4), channel_id=1, replica_groups={{264,268,256,260,328,332,320,324,392,396,384,388,456,460,448,452,8,12,0..., dimensions={0} | all-to-all | bytes 163840 | tf_op jit(solution)/shard_map/all_to_all | solution.py:261
  52.4 0.1 reduce_sum.19
  52.5 9.6 %all_to_all.36 = f32[16,1,640]{2,1,0:T(1,128)S(1)} all-to-all(f32[16,1,640]{2,1,0:T(1,128)S(1)} %broadcast_in_dim.5), channel_id=1, replica_groups={{18,19,16,17,2,3,0,1,50,51,48,49,34,35,32,33},{22,23,20,21,6,7,4,5,54,5..., dimensions={0} | all-to-all | bytes 81920 | tf_op jit(solution)/shard_map/all_to_all | solution.py:261
  62.2 0.8 %finish.1 = (f32[8,128]{1,0:T(8,128)}, f32[4,80]{1,0:T(4,128)}) custom-call(f32[80,128]{1,0:T(8,128)S(1)} %bitcast.6, bf16[80,1024]{1,0:T(8,128)(2,1)S(1)} %copy-done, bf16[128,1024]{1,0:T(8,128)(2,1)S(1)} %all_to_all.26.modes_ref), custom_call_target="tpu_custom_call" | custom-call | tf_op jit(solution)/shard_map/finish/pallas_call | solution.py:230
  (3 shorter events, 0.1 us)
Async XLA Ops:
  1.7 27.0 %copy-start = (bf16[80,1024]{1,0:T(8,128)(2,1)S(1)}, bf16[80,1024]{1,0:T(8,128)(2,1)}, u32[]{:S(2)}) copy-start(bf16[80,1024]{1,0:T(8,128)(2,1)} %members_ref.3) | copy-start | bytes 491524
  5.2 23.4 %all-to-all-start = ((bf16[4,32,1024]{2,0,1:T(4,128)(2,1)}), bf16[4,32,1024]{2,0,1:T(4,128)(2,1)S(1)}, u32[]{:S(2)}, u32[]{:S(2)}) async-start(bf16[4,32,1024]{2,0,1:T(4,128)(2,1)} %bitcast), calls=%async_computation | async-start | bytes 524288 | tf_op jit(solution)/shard_map/all_to_all | solution.py:275
  21.7 7.0 %collective-permute-start = (f32[1,128]{1,0:T(1,128)S(1)}, f32[1,128]{1,0:T(1,128)S(1)}, u32[]{:S(2)}, u32[]{:S(2)}) collective-permute-start(f32[1,128]{1,0:T(1,128)S(1)} %get-tuple-element.16), channel_id=1, source_target_pairs={{0,32},{31,511},{32,64},{63,31},{64,96},{95,63},{96,128},{127,95},... | collective-permute-start | bytes 1544 | tf_op jit(solution)/shard_map/ppermute | solution.py:284

commit v5 on v1

--- a/solution.py
+++ b/solution.py
@@ -112,7 +112,7 @@
 
 
 def waits_long():
-    return lax.axis_index("zhi") < lax.axis_size("zhi") // 2
+    return lax.axis_index("zhi") < lax.axis_size("zhi") // 4
 
 
 def early_kernel(last, modes_ref, begin_ref, innov_ref, obs_ref, laid_ref, own_ref, halo_ref, lay_sems, *scratch):

time: 63.2 us -> 63.2 us (level)
  no operation moved by 1% of the time
where the time goes in v5:
time: 63.2 us; the launch traced here: 62.9 us
  blocking collectives  34 us (54%)
  starting transfers between devices  17 us (27%)
  waiting for transfers between devices  6.24 us (10%)
  Pallas kernels  4.63 us (7%)
  between operations  0.71 us (1%)
    all_to_all x3, blocking collectives, exchange(): lax.all_to_all(x, axis, split_axis=0, concat_axis=0, axis_index_groups=pl...  34 us
    all_to_all x1, starting transfers between devices, on_device(): lax.all_to_all(laid, MODE, split_axis=1, concat_axis=0, axis_index_groups...  16.3 us
    all_to_all x1, waiting for transfers between devices, on_device(): lax.all_to_all(laid, MODE, split_axis=1, concat_axis=0, axis_index_groups...  6.24 us
    pallas_call x1, Pallas kernels, early(): pl.pallas_call(functools.partial(early_kernel, last), out_shape=(jax.Shap...  3.37 us
  transfers between devices with their start and end apart: 2, of which 1 were waited for; matrix products, arithmetic and copies ran while one was open for 0% of the time, Pallas kernels for 0%

profile of v5, /device:TPU:1, one launch (start us, length us, event | category | flops | bytes accessed | tf_op | source)
XLA Modules:
  0.0 62.9 jit_solution(10647998356640091901)
XLA Ops:
  0.6 0.0 copy-start
  0.6 3.4 %early.1 = (bf16[4,32768]{1,0:T(4,128)(2,1)}, f32[8,128]{1,0:T(8,128)S(1)}, f32[1,128]{1,0:T(1,128)S(1)}) custom-call(bf16[4,32768]{1,0:T(4,128)(2,1)} %modes_ref.1, s32[128]{0:T(128)} %begin_ref.3, f32[128,128]{1,0:T(8,128)} %innov_ref.3, bf16[128,128,128]{2,1,0:T(8,128)(2,1)} %obs_ref.3), custom_call_target="tpu_custom_call" | custom-call | tf_op jit(solution)/shard_map/early/pallas_call | solution.py:171
  4.0 16.3 %all-to-all-start = ((bf16[4,32,1024]{2,0,1:T(4,128)(2,1)}), bf16[4,32,1024]{2,0,1:T(4,128)(2,1)S(1)}, u32[]{:S(2)}, u32[]{:S(2)}) async-start(bf16[4,32,1024]{2,0,1:T(4,128)(2,1)} %bitcast), calls=%async_computation | async-start | bytes 524288 | tf_op jit(solution)/shard_map/all_to_all | solution.py:286
  20.4 0.1 late.1
  20.5 0.7 %collective-permute-start = (f32[1,128]{1,0:T(1,128)S(1)}, f32[1,128]{1,0:T(1,128)S(1)}, u32[]{:S(2)}, u32[]{:S(2)}) collective-permute-start(f32[1,128]{1,0:T(1,128)S(1)} %get-tuple-element.12), channel_id=1, source_target_pairs={{0,32},{31,511},{32,64},{63,31},{64,96},{95,63},{96,128},{127,95},... | collective-permute-start | bytes 1544 | tf_op jit(solution)/shard_map/ppermute | solution.py:295
  21.2 6.2 %all-to-all-done = bf16[4,32,1024]{2,0,1:T(4,128)(2,1)S(1)} async-done(((bf16[4,32,1024]{2,0,1:T(4,128)(2,1)}), bf16[4,32,1024]{2,0,1:T(4,128)(2,1)S(1)}, u32[]{:S(2)}, u32[]{:S(2)}) %all-to-all-start) | async-done | bytes 262176 | tf_op jit(solution)/shard_map/all_to_all | solution.py:286
  27.4 0.1 all_to_all.26.modes_ref
  27.5 0.0 collective-permute-done.halo_ref
  27.5 0.0 copy-done
  27.5 0.3 project.1
  27.8 8.7 %all_to_all.34 = f32[16,1,640]{2,1,0:T(1,128)S(1)} all-to-all(f32[16,1,640]{2,1,0:T(1,128)S(1)} %bitcast.7), channel_id=1, replica_groups={{18,19,16,17,2,3,0,1,50,51,48,49,34,35,32,33},{22,23,20,21,6,7,4,5,54,5..., dimensions={0} | all-to-all | bytes 81920 | tf_op jit(solution)/shard_map/all_to_all | solution.py:274
  36.5 15.7 %all_to_all.35 = f32[32,1,640]{2,1,0:T(1,128)S(1)} all-to-all(f32[32,1,640]{2,1,0:T(1,128)S(1)} %broadcast_in_dim.4), channel_id=1, replica_groups={{264,268,256,260,328,332,320,324,392,396,384,388,456,460,448,452,8,12,0..., dimensions={0} | all-to-all | bytes 163840 | tf_op jit(solution)/shard_map/all_to_all | solution.py:274
  52.3 0.1 reduce_sum.19
  52.4 9.6 %all_to_all.36 = f32[16,1,640]{2,1,0:T(1,128)S(1)} all-to-all(f32[16,1,640]{2,1,0:T(1,128)S(1)} %broadcast_in_dim.5), channel_id=1, replica_groups={{18,19,16,17,2,3,0,1,50,51,48,49,34,35,32,33},{22,23,20,21,6,7,4,5,54,5..., dimensions={0} | all-to-all | bytes 81920 | tf_op jit(solution)/shard_map/all_to_all | solution.py:274
  62.0 0.8 %finish.1 = (f32[8,128]{1,0:T(8,128)}, f32[4,80]{1,0:T(4,128)}) custom-call(f32[80,128]{1,0:T(8,128)S(1)} %bitcast.6, bf16[80,1024]{1,0:T(8,128)(2,1)S(1)} %copy-done, bf16[128,1024]{1,0:T(8,128)(2,1)S(1)} %all_to_all.26.modes_ref), custom_call_target="tpu_custom_call" | custom-call | tf_op jit(solution)/shard_map/finish/pallas_call | solution.py:243
  (3 shorter events, 0.1 us)
Async XLA Ops:
  0.6 26.9 %copy-start = (bf16[80,1024]{1,0:T(8,128)(2,1)S(1)}, bf16[80,1024]{1,0:T(8,128)(2,1)}, u32[]{:S(2)}) copy-start(bf16[80,1024]{1,0:T(8,128)(2,1)} %members_ref.3) | copy-start | bytes 491524
  4.0 23.4 %all-to-all-start = ((bf16[4,32,1024]{2,0,1:T(4,128)(2,1)}), bf16[4,32,1024]{2,0,1:T(4,128)(2,1)S(1)}, u32[]{:S(2)}, u32[]{:S(2)}) async-start(bf16[4,32,1024]{2,0,1:T(4,128)(2,1)} %bitcast), calls=%async_computation | async-start | bytes 524288 | tf_op jit(solution)/shard_map/all_to_all | solution.py:286
  20.5 7.0 %collective-permute-start = (f32[1,128]{1,0:T(1,128)S(1)}, f32[1,128]{1,0:T(1,128)S(1)}, u32[]{:S(2)}, u32[]{:S(2)}) collective-permute-start(f32[1,128]{1,0:T(1,128)S(1)} %get-tuple-element.12), channel_id=1, source_target_pairs={{0,32},{31,511},{32,64},{63,31},{64,96},{95,63},{96,128},{127,95},... | collective-permute-start | bytes 1544 | tf_op jit(solution)/shard_map/ppermute | solution.py:295

commit v6 on v5

--- a/solution.py
+++ b/solution.py
@@ -112,7 +112,7 @@
 
 
 def waits_long():
-    return lax.axis_index("zhi") < lax.axis_size("zhi") // 4
+    return (lax.axis_index("zhi") == 0) & (lax.axis_index("zlo") == 0)
 
 
 def early_kernel(last, modes_ref, begin_ref, innov_ref, obs_ref, laid_ref, own_ref, halo_ref, lay_sems, *scratch):

time: 63.2 us -> 63.2 us (level)
  no operation moved by 1% of the time
where the time goes in v6:
time: 63.2 us; the launch traced here: 62.9 us
  blocking collectives  34 us (54%)
  starting transfers between devices  16.8 us (27%)
  waiting for transfers between devices  6.24 us (10%)
  Pallas kernels  4.85 us (8%)
  between operations  0.71 us (1%)
    all_to_all x3, blocking collectives, exchange(): lax.all_to_all(x, axis, split_axis=0, concat_axis=0, axis_index_groups=pl...  34 us
    all_to_all x1, starting transfers between devices, on_device(): lax.all_to_all(laid, MODE, split_axis=1, concat_axis=0, axis_index_groups...  16.1 us
    all_to_all x1, waiting for transfers between devices, on_device(): lax.all_to_all(laid, MODE, split_axis=1, concat_axis=0, axis_index_groups...  6.24 us
    pallas_call x1, Pallas kernels, early(): pl.pallas_call(functools.partial(early_kernel, last), out_shape=(jax.Shap...  3.6 us
  transfers between devices with their start and end apart: 2, of which 1 were waited for; matrix products, arithmetic and copies ran while one was open for 0% of the time, Pallas kernels for 0%

profile of v6, /device:TPU:1, one launch (start us, length us, event | category | flops | bytes accessed | tf_op | source)
XLA Modules:
  0.0 62.9 jit_solution(4529918494533353706)
XLA Ops:
  0.6 0.0 copy-start
  0.6 3.6 %early.1 = (bf16[4,32768]{1,0:T(4,128)(2,1)}, f32[8,128]{1,0:T(8,128)S(1)}, f32[1,128]{1,0:T(1,128)S(1)}) custom-call(bf16[4,32768]{1,0:T(4,128)(2,1)} %modes_ref.1, s32[128]{0:T(128)} %begin_ref.3, f32[128,128]{1,0:T(8,128)} %innov_ref.3, bf16[128,128,128]{2,1,0:T(8,128)(2,1)} %obs_ref.3), custom_call_target="tpu_custom_call" | custom-call | tf_op jit(solution)/shard_map/early/pallas_call | solution.py:171
  4.2 16.1 %all-to-all-start = ((bf16[4,32,1024]{2,0,1:T(4,128)(2,1)}), bf16[4,32,1024]{2,0,1:T(4,128)(2,1)S(1)}, u32[]{:S(2)}, u32[]{:S(2)}) async-start(bf16[4,32,1024]{2,0,1:T(4,128)(2,1)} %bitcast), calls=%async_computation | async-start | bytes 524288 | tf_op jit(solution)/shard_map/all_to_all | solution.py:286
  20.4 0.1 late.1
  20.5 0.7 %collective-permute-start = (f32[1,128]{1,0:T(1,128)S(1)}, f32[1,128]{1,0:T(1,128)S(1)}, u32[]{:S(2)}, u32[]{:S(2)}) collective-permute-start(f32[1,128]{1,0:T(1,128)S(1)} %get-tuple-element.12), channel_id=1, source_target_pairs={{0,32},{31,511},{32,64},{63,31},{64,96},{95,63},{96,128},{127,95},... | collective-permute-start | bytes 1544 | tf_op jit(solution)/shard_map/ppermute | solution.py:295
  21.2 6.2 %all-to-all-done = bf16[4,32,1024]{2,0,1:T(4,128)(2,1)S(1)} async-done(((bf16[4,32,1024]{2,0,1:T(4,128)(2,1)}), bf16[4,32,1024]{2,0,1:T(4,128)(2,1)S(1)}, u32[]{:S(2)}, u32[]{:S(2)}) %all-to-all-start) | async-done | bytes 262176 | tf_op jit(solution)/shard_map/all_to_all | solution.py:286
  27.4 0.1 all_to_all.26.modes_ref
  27.5 0.0 collective-permute-done.halo_ref
  27.5 0.0 copy-done
  27.5 0.3 project.1
  27.8 8.7 %all_to_all.34 = f32[16,1,640]{2,1,0:T(1,128)S(1)} all-to-all(f32[16,1,640]{2,1,0:T(1,128)S(1)} %bitcast.7), channel_id=1, replica_groups={{18,19,16,17,2,3,0,1,50,51,48,49,34,35,32,33},{22,23,20,21,6,7,4,5,54,5..., dimensions={0} | all-to-all | bytes 81920 | tf_op jit(solution)/shard_map/all_to_all | solution.py:274
  36.5 15.7 %all_to_all.35 = f32[32,1,640]{2,1,0:T(1,128)S(1)} all-to-all(f32[32,1,640]{2,1,0:T(1,128)S(1)} %broadcast_in_dim.4), channel_id=1, replica_groups={{264,268,256,260,328,332,320,324,392,396,384,388,456,460,448,452,8,12,0..., dimensions={0} | all-to-all | bytes 163840 | tf_op jit(solution)/shard_map/all_to_all | solution.py:274
  52.3 0.1 reduce_sum.19
  52.4 9.6 %all_to_all.36 = f32[16,1,640]{2,1,0:T(1,128)S(1)} all-to-all(f32[16,1,640]{2,1,0:T(1,128)S(1)} %broadcast_in_dim.5), channel_id=1, replica_groups={{18,19,16,17,2,3,0,1,50,51,48,49,34,35,32,33},{22,23,20,21,6,7,4,5,54,5..., dimensions={0} | all-to-all | bytes 81920 | tf_op jit(solution)/shard_map/all_to_all | solution.py:274
  62.0 0.8 %finish.1 = (f32[8,128]{1,0:T(8,128)}, f32[4,80]{1,0:T(4,128)}) custom-call(f32[80,128]{1,0:T(8,128)S(1)} %bitcast.6, bf16[80,1024]{1,0:T(8,128)(2,1)S(1)} %copy-done, bf16[128,1024]{1,0:T(8,128)(2,1)S(1)} %all_to_all.26.modes_ref), custom_call_target="tpu_custom_call" | custom-call | tf_op jit(solution)/shard_map/finish/pallas_call | solution.py:243
  (3 shorter events, 0.1 us)
Async XLA Ops:
  0.6 26.9 %copy-start = (bf16[80,1024]{1,0:T(8,128)(2,1)S(1)}, bf16[80,1024]{1,0:T(8,128)(2,1)}, u32[]{:S(2)}) copy-start(bf16[80,1024]{1,0:T(8,128)(2,1)} %members_ref.3) | copy-start | bytes 491524
  4.2 23.2 %all-to-all-start = ((bf16[4,32,1024]{2,0,1:T(4,128)(2,1)}), bf16[4,32,1024]{2,0,1:T(4,128)(2,1)S(1)}, u32[]{:S(2)}, u32[]{:S(2)}) async-start(bf16[4,32,1024]{2,0,1:T(4,128)(2,1)} %bitcast), calls=%async_computation | async-start | bytes 524288 | tf_op jit(solution)/shard_map/all_to_all | solution.py:286
  20.5 7.0 %collective-permute-start = (f32[1,128]{1,0:T(1,128)S(1)}, f32[1,128]{1,0:T(1,128)S(1)}, u32[]{:S(2)}, u32[]{:S(2)}) collective-permute-start(f32[1,128]{1,0:T(1,128)S(1)} %get-tuple-element.12), channel_id=1, source_target_pairs={{0,32},{31,511},{32,64},{63,31},{64,96},{95,63},{96,128},{127,95},... | collective-permute-start | bytes 1544 | tf_op jit(solution)/shard_map/ppermute | solution.py:295

commit v7 on v5

--- a/solution.py
+++ b/solution.py
@@ -27,7 +27,7 @@
 SPACE = ("y", "xlo")
 NEAR = ("xlo", "xhi", "zlo", "core")
 FAR = ("y", "zhi")
-FIRST = {NEAR: {"xhi": 1, "zlo": 1}, FAR: {"y": 4, "zhi": 2}, MODE: {"xhi": 1, "zhi": 2}}
+FIRST = {NEAR: {"xhi": 1, "zlo": 1}, FAR: {"y": 4, "zhi": 3}, MODE: {"xhi": 1, "zhi": 2}}
 
 
 def mode_index():

time: 63.2 us -> 64.3 us (1.017)
  blocking collectives: 34 us -> 35 us
    all_to_all x3, blocking collectives: 34 us -> 35 us  [exchange(): lax.all_to_all(x, axis, split_axis=0, concat_axis=0, axis_index_groups=pl...]
where the time goes in v7:
time: 64.3 us; the launch traced here: 64 us
  blocking collectives  35 us (54%)
  starting transfers between devices  17 us (26%)
  waiting for transfers between devices  6.24 us (10%)
  Pallas kernels  4.87 us (8%)
  between operations  0.71 us (1%)
    all_to_all x3, blocking collectives, exchange(): lax.all_to_all(x, axis, split_axis=0, concat_axis=0, axis_index_groups=pl...  35 us
    all_to_all x1, starting transfers between devices, on_device(): lax.all_to_all(laid, MODE, split_axis=1, concat_axis=0, axis_index_groups...  16.3 us
    all_to_all x1, waiting for transfers between devices, on_device(): lax.all_to_all(laid, MODE, split_axis=1, concat_axis=0, axis_index_groups...  6.24 us
    pallas_call x1, Pallas kernels, early(): pl.pallas_call(functools.partial(early_kernel, last), out_shape=(jax.Shap...  3.61 us
  transfers between devices with their start and end apart: 2, of which 1 were waited for; matrix products, arithmetic and copies ran while one was open for 0% of the time, Pallas kernels for 0%

profile of v7, /device:TPU:1, one launch (start us, length us, event | category | flops | bytes accessed | tf_op | source)
XLA Modules:
  0.0 64.0 jit_solution(1204869747592946050)
XLA Ops:
  0.6 0.0 copy-start
  0.6 3.6 %early.1 = (bf16[4,32768]{1,0:T(4,128)(2,1)}, f32[8,128]{1,0:T(8,128)S(1)}, f32[1,128]{1,0:T(1,128)S(1)}) custom-call(bf16[4,32768]{1,0:T(4,128)(2,1)} %modes_ref.1, s32[128]{0:T(128)} %begin_ref.3, f32[128,128]{1,0:T(8,128)} %innov_ref.3, bf16[128,128,128]{2,1,0:T(8,128)(2,1)} %obs_ref.3), custom_call_target="tpu_custom_call" | custom-call | tf_op jit(solution)/shard_map/early/pallas_call | solution.py:171
  4.3 16.3 %all-to-all-start = ((bf16[4,32,1024]{2,0,1:T(4,128)(2,1)}), bf16[4,32,1024]{2,0,1:T(4,128)(2,1)S(1)}, u32[]{:S(2)}, u32[]{:S(2)}) async-start(bf16[4,32,1024]{2,0,1:T(4,128)(2,1)} %bitcast), calls=%async_computation | async-start | bytes 524288 | tf_op jit(solution)/shard_map/all_to_all | solution.py:286
  20.6 0.1 late.1
  20.7 0.7 %collective-permute-start = (f32[1,128]{1,0:T(1,128)S(1)}, f32[1,128]{1,0:T(1,128)S(1)}, u32[]{:S(2)}, u32[]{:S(2)}) collective-permute-start(f32[1,128]{1,0:T(1,128)S(1)} %get-tuple-element.12), channel_id=1, source_target_pairs={{0,32},{31,511},{32,64},{63,31},{64,96},{95,63},{96,128},{127,95},... | collective-permute-start | bytes 1544 | tf_op jit(solution)/shard_map/ppermute | solution.py:295
  21.4 6.2 %all-to-all-done = bf16[4,32,1024]{2,0,1:T(4,128)(2,1)S(1)} async-done(((bf16[4,32,1024]{2,0,1:T(4,128)(2,1)}), bf16[4,32,1024]{2,0,1:T(4,128)(2,1)S(1)}, u32[]{:S(2)}, u32[]{:S(2)}) %all-to-all-start) | async-done | bytes 262176 | tf_op jit(solution)/shard_map/all_to_all | solution.py:286
  27.6 0.1 all_to_all.26.modes_ref
  27.7 0.0 collective-permute-done.halo_ref
  27.7 0.0 copy-done
  27.7 0.3 project.1
  28.0 8.5 %all_to_all.34 = f32[16,1,640]{2,1,0:T(1,128)S(1)} all-to-all(f32[16,1,640]{2,1,0:T(1,128)S(1)} %bitcast.7), channel_id=1, replica_groups={{18,19,16,17,2,3,0,1,50,51,48,49,34,35,32,33},{22,23,20,21,6,7,4,5,54,5..., dimensions={0} | all-to-all | bytes 81920 | tf_op jit(solution)/shard_map/all_to_all | solution.py:274
  36.6 16.6 %all_to_all.35 = f32[32,1,640]{2,1,0:T(1,128)S(1)} all-to-all(f32[32,1,640]{2,1,0:T(1,128)S(1)} %broadcast_in_dim.4), channel_id=1, replica_groups={{268,256,260,264,332,320,324,328,396,384,388,392,460,448,452,456,12,0,4..., dimensions={0} | all-to-all | bytes 163840 | tf_op jit(solution)/shard_map/all_to_all | solution.py:274
  53.3 0.1 reduce_sum.19
  53.4 9.8 %all_to_all.36 = f32[16,1,640]{2,1,0:T(1,128)S(1)} all-to-all(f32[16,1,640]{2,1,0:T(1,128)S(1)} %broadcast_in_dim.5), channel_id=1, replica_groups={{18,19,16,17,2,3,0,1,50,51,48,49,34,35,32,33},{22,23,20,21,6,7,4,5,54,5..., dimensions={0} | all-to-all | bytes 81920 | tf_op jit(solution)/shard_map/all_to_all | solution.py:274
  63.2 0.8 %finish.1 = (f32[8,128]{1,0:T(8,128)}, f32[4,80]{1,0:T(4,128)}) custom-call(f32[80,128]{1,0:T(8,128)S(1)} %bitcast.6, bf16[80,1024]{1,0:T(8,128)(2,1)S(1)} %copy-done, bf16[128,1024]{1,0:T(8,128)(2,1)S(1)} %all_to_all.26.modes_ref), custom_call_target="tpu_custom_call" | custom-call | tf_op jit(solution)/shard_map/finish/pallas_call | solution.py:243
  (3 shorter events, 0.1 us)
Async XLA Ops:
  0.6 27.1 %copy-start = (bf16[80,1024]{1,0:T(8,128)(2,1)S(1)}, bf16[80,1024]{1,0:T(8,128)(2,1)}, u32[]{:S(2)}) copy-start(bf16[80,1024]{1,0:T(8,128)(2,1)} %members_ref.3) | copy-start | bytes 491524
  4.3 23.4 %all-to-all-start = ((bf16[4,32,1024]{2,0,1:T(4,128)(2,1)}), bf16[4,32,1024]{2,0,1:T(4,128)(2,1)S(1)}, u32[]{:S(2)}, u32[]{:S(2)}) async-start(bf16[4,32,1024]{2,0,1:T(4,128)(2,1)} %bitcast), calls=%async_computation | async-start | bytes 524288 | tf_op jit(solution)/shard_map/all_to_all | solution.py:286
  20.7 7.0 %collective-permute-start = (f32[1,128]{1,0:T(1,128)S(1)}, f32[1,128]{1,0:T(1,128)S(1)}, u32[]{:S(2)}, u32[]{:S(2)}) collective-permute-start(f32[1,128]{1,0:T(1,128)S(1)} %get-tuple-element.12), channel_id=1, source_target_pairs={{0,32},{31,511},{32,64},{63,31},{64,96},{95,63},{96,128},{127,95},... | collective-permute-start | bytes 1544 | tf_op jit(solution)/shard_map/ppermute | solution.py:295
